TPU v7x, 32 devices: a whole 2x2x4 slice. The times are simulated.
32 devices in a mesh: grp: 2 (over y), row: 4 (over z), col: 2 (over x), sub: 2 (over core).
Axes of the slice: x: 2, y: 2, z: 4, core: 2. Of those that a mesh axis runs over, the one named last changes fastest.
Arguments:
- filament_slot: int32 [16384], P(('grp', 'row', 'col', 'sub')), parts along dimension 0, may hold values from 0 to 8191, each once
- wire_radius: float32 [16384], P(('grp', 'row', 'col', 'sub')), parts along dimension 0, may hold values from 0.02 to 0.05
- strand_radius: float32 [128], P('grp'), parts along dimension 0, may hold values from 0.2 to 1
- test_matrix: float32 [64, 16384], P(None, ('grp', 'row', 'col', 'sub')), parts along dimension 1, may hold values from -6 to 6
Outputs:
- ortho_basis: float32 [64, 16384], P(None, ('grp', 'row', 'col', 'sub')), parts along dimension 1
- sketch_factor: float32 [128, 64], P('grp'), parts along dimension 0
There are 2 independent parts, one for each index of `grp`. A program takes and returns all parts, laid end to end along the dimension named above; each array names one. Nothing has to cross between parts.
Inputs may be any that keep to these rules, and one draw needn't show every extreme that they name: `filament_slot`: every number from 0 to 8191 occurs exactly once.
All inputs are finite; a program needn't handle non-finite values.
Results may differ from a plain program's by a relative error of at most 0.0005.
Values sent between devices are 32-bit elements; how exact they have to be, the bound alone decides.
A program may use at most 64 MiB of HBM per device.

v0:
```python
import math
import jax
import jax.numpy as jnp
from jax import lax
from jax.sharding import PartitionSpec as P

SEGMENTS = 128
mu_scale = 1e-05
twist_rate = 4.0 * math.pi


def from_behind(shard, axis, by):
    count = lax.axis_size(axis)
    return lax.ppermute(shard, axis, [(i, (i + by) % count) for i in range(count)])


def filament_geometry(filament_slot, wire_radius, strand_radius):
    strand = filament_slot // SEGMENTS
    segment = filament_slot % SEGMENTS
    strand_count = strand_radius.shape[0]
    onehot = (strand[None, :] == jnp.arange(strand_count, dtype=jnp.int32)[:, None]).astype(
        jnp.float32
    )
    radius = jnp.sum(onehot * strand_radius[:, None], axis=0)
    phase = 2.0 * math.pi / strand_count * strand.astype(jnp.float32)
    height = (segment.astype(jnp.float32) + 0.5) / SEGMENTS
    twist_angle = phase + twist_rate * height
    cosine_part = jnp.cos(twist_angle)
    sine_part = jnp.sin(twist_angle)
    return jnp.stack(
        [
            radius * cosine_part,
            radius * sine_part,
            height,
            -twist_rate * radius * sine_part,
            twist_rate * radius * cosine_part,
            jnp.ones_like(height),
            wire_radius * wire_radius,
        ]
    )


def source_block(targets, sources, columns):
    delta_x = sources[0][:, None] - targets[0][None, :]
    delta_y = sources[1][:, None] - targets[1][None, :]
    delta_z = sources[2][:, None] - targets[2][None, :]
    distance = (
        delta_x * delta_x
        + delta_y * delta_y
        + delta_z * delta_z
        + sources[6][:, None]
        + targets[6][None, :]
    )
    alignment = (
        sources[3][:, None] * targets[3][None, :]
        + sources[4][:, None] * targets[4][None, :]
        + sources[5][:, None] * targets[5][None, :]
    )
    kernel = mu_scale * alignment * lax.rsqrt(distance)
    return jnp.dot(
        columns, kernel, precision=lax.Precision.HIGHEST, preferred_element_type=jnp.float32
    )


def sweep_sources(targets, sources, columns):
    source_count = sources.shape[1]
    block_len = math.gcd(source_count, 2048)
    block_count = source_count // block_len
    if block_count == 1:
        return source_block(targets, sources, columns)

    def add_block(block_index, running):
        offset = block_index * block_len
        geo_part = lax.dynamic_slice_in_dim(sources, offset, block_len, 1)
        col_part = lax.dynamic_slice_in_dim(columns, offset, block_len, 1)
        return running + source_block(targets, geo_part, col_part)

    initial = jnp.zeros((columns.shape[0], targets.shape[1]), jnp.float32)
    return lax.fori_loop(0, block_count, add_block, initial)


def per_device(filament_slot, wire_radius, strand_radius, test_matrix):
    targets = filament_geometry(filament_slot, wire_radius, strand_radius)
    geo_row, col_row = (
        lax.all_gather(targets, ("col", "sub"), axis=1, tiled=True),
        lax.all_gather(test_matrix, ("col", "sub"), axis=1, tiled=True),
    )
    sketch = sweep_sources(targets, geo_row, col_row)
    half_cycle = lax.axis_size("row") // 2

    def both_ways(turn_index, state_now):
        running, ahead_geo, ahead_cols, behind_geo, behind_cols = state_now
        ahead_geo, ahead_cols = from_behind((ahead_geo, ahead_cols), "row", 1)
        behind_geo, behind_cols = from_behind((behind_geo, behind_cols), "row", -1)
        running = running + sweep_sources(targets, ahead_geo, ahead_cols)
        running = running + sweep_sources(targets, behind_geo, behind_cols)
        return (running, ahead_geo, ahead_cols, behind_geo, behind_cols)

    state_end = lax.fori_loop(
        1, half_cycle, both_ways, (sketch, geo_row, col_row, geo_row, col_row)
    )
    far_geo, far_cols = from_behind((state_end[1], state_end[2]), "row", 1)
    sketch = state_end[0] + sweep_sources(targets, far_geo, far_cols)
    local_gram = jnp.dot(
        sketch, sketch.T, precision=lax.Precision.HIGHEST, preferred_element_type=jnp.float32
    )
    gram_matrix = lax.psum(local_gram, ("row", "col", "sub"))
    cholesky_low = jnp.linalg.cholesky(gram_matrix)
    solved = jax.scipy.linalg.solve_triangular(cholesky_low, sketch, lower=True)
    filament_total = (
        sketch.shape[1] * lax.axis_size("row") * lax.axis_size("col") * lax.axis_size("sub")
    )
    scale_root = math.sqrt(filament_total)
    return (solved * scale_root, cholesky_low.T / scale_root)


def solution(mesh):
    return jax.shard_map(
        per_device,
        mesh=mesh,
        in_specs=(
            P(("grp", "row", "col", "sub")),
            P(("grp", "row", "col", "sub")),
            P("grp"),
            P(None, ("grp", "row", "col", "sub")),
        ),
        out_specs=(P(None, ("grp", "row", "col", "sub")), P("grp", None)),
        check_vma=False,
    )
```

profile of v0, /device:TPU:0, one launch (start us, length us, event | category | flops | bytes accessed | tf_op | source)
XLA Modules:
  0.0 137.8 jit_solution(15863045663286231874)
XLA Ops:
  0.6 0.0 copy-start.1
  0.6 0.0 copy-start
  0.7 9.0 %all_gather.7 = f32[64,2048]{1,0:T(8,128)S(1)} all-gather(f32[64,512]{1,0:T(8,128)} %param.7), channel_id=1, replica_groups=mesh['grp'=2,'row'=4,'col'=2,'sub'=2] {'col','sub'}, dimensions={1}, use_global_device_ids=true | all-gather | bytes 655360 | tf_op jit(solution)/shard_map/all_gather | solution.py:86
  9.6 3.6 %collective-permute-start.3 = (f32[64,2048]{1,0:T(8,128)S(1)}, f32[64,2048]{1,0:T(8,128)S(1)}, u32[]{:S(2)}, u32[]{:S(2)}) collective-permute-start(f32[64,2048]{1,0:T(8,128)S(1)} %all_gather.7), channel_id=1, source_target_pairs={{0,12},{4,0},{8,4},{12,8},{1,13},{5,1},{9,5},{13,9},{2,14},{6,2},{... | collective-permute-start | bytes 1572872 | tf_op jit(solution)/shard_map/while/body/eval_jaxpr/ppermute | solution.py:14
  13.2 0.0 collective-permute-start.1
  13.2 0.1 fusion.146
  13.3 0.0 copy-done.2
  13.3 0.1 select_reduce_fusion
  13.5 5.2 %all_gather.6 = f32[7,2048]{1,0:T(8,128)S(1)} all-gather(f32[7,512]{1,0:T(8,128)S(1)} %stack.27), channel_id=1, replica_groups=mesh['grp'=2,'row'=4,'col'=2,'sub'=2] {'col','sub'}, dimensions={1}, use_global_device_ids=true | all-gather | bytes 71680 | tf_op jit(solution)/shard_map/all_gather | solution.py:85
  18.8 3.8 %collective-permute-start.2 = (f32[7,2048]{1,0:T(8,128)S(1)}, f32[7,2048]{1,0:T(8,128)S(1)}, u32[]{:S(2)}, u32[]{:S(2)}) collective-permute-start(f32[7,2048]{1,0:T(8,128)S(1)} %all_gather.6), channel_id=1, source_target_pairs={{0,12},{4,0},{8,4},{12,8},{1,13},{5,1},{9,5},{13,9},{2,14},{6,2},{... | collective-permute-start | bytes 172040 | tf_op jit(solution)/shard_map/while/body/eval_jaxpr/ppermute | solution.py:14
  22.6 0.0 collective-permute-start
  22.6 5.4 %fusion.54 = f32[512,64]{0,1:T(8,128)S(1)} fusion(f32[64,2048]{1,0:T(8,128)S(1)} %all_gather.7, f32[512]{0:T(512)S(1)} %mul.293, f32[2048]{0:T(1024)S(1)} %bitcast.74, f32[512]{0:T(512)S(1)} %get-tuple-element.81, f32[2048]{0:T(1024)S(1)} %bitcast.75, f32[512]{0:T(512)S(1)} %get-tuple-element.79, f32[2048]{0:T(1024)S(1)} %bitcast.76, ...), kind=kOutput, calls=%fused_computation.54 | convolution fusion | flops 822083584 | bytes 724992 | tf_op jit(solution)/shard_map/dot_general | solution.py:60
  28.0 11.9 %collective-permute-done = f32[7,2048]{1,0:T(8,128)S(1)} collective-permute-done((f32[7,2048]{1,0:T(8,128)S(1)}, f32[7,2048]{1,0:T(8,128)S(1)}, u32[]{:S(2)}, u32[]{:S(2)}) %collective-permute-start) | collective-permute-done | bytes 57376 | tf_op jit(solution)/shard_map/while/body/eval_jaxpr/ppermute | solution.py:14
  40.0 1.6 %collective-permute-start.4 = (f32[7,2048]{1,0:T(8,128)S(1)}, f32[7,2048]{1,0:T(8,128)S(1)}, u32[]{:S(2)}, u32[]{:S(2)}) collective-permute-start(f32[7,2048]{1,0:T(8,128)S(1)} %collective-permute-done), channel_id=1, source_target_pairs={{0,4},{4,8},{8,12},{12,0},{1,5},{5,9},{9,13},{13,1},{2,6},{6,10},{... | collective-permute-start | bytes 172040 | tf_op jit(solution)/shard_map/ppermute | solution.py:14
  41.6 0.0 collective-permute-done.2
  41.6 4.4 %collective-permute-done.4 = f32[7,2048]{1,0:T(8,128)S(1)} collective-permute-done((f32[7,2048]{1,0:T(8,128)S(1)}, f32[7,2048]{1,0:T(8,128)S(1)}, u32[]{:S(2)}, u32[]{:S(2)}) %collective-permute-start.4) | collective-permute-done | bytes 57376 | tf_op jit(solution)/shard_map/ppermute | solution.py:14
  46.1 0.0 collective-permute-done.1
  46.1 0.2 collective-permute-start.5
  46.4 0.0 collective-permute-done.3
  46.4 5.5 %fusion.18 = f32[512,64]{0,1:T(8,128)S(1)} fusion(f32[64,2048]{1,0:T(8,128)S(1)} %collective-permute-done.3, f32[2048]{0:T(1024)S(1)} %bitcast.67, f32[2048]{0:T(1024)S(1)} %bitcast.68, f32[2048]{0:T(1024)S(1)} %bitcast.69, f32[2048]{0:T(1024)S(1)} %bitcast.70, f32[2048]{0:T(1024)S(1)} %bitcast.71, f32[2048]{0:T(1024)S(1)} %bitcast.72, ...), kind=kOutput, calls=%fused_computation.18 | convolution fusion | flops 822083584 | bytes 724992 | tf_op jit(solution)/shard_map/while/body/eval_jaxpr/dot_general | solution.py:60
  51.9 5.5 %fusion.131 = f32[512,64]{0,1:T(8,128)S(1)} fusion(f32[512,64]{0,1:T(8,128)S(1)} %fusion.18, f32[512,64]{0,1:T(8,128)S(1)} %fusion.54, f32[64,2048]{1,0:T(8,128)S(1)} %collective-permute-done.1, f32[2048]{0:T(1024)S(1)} %bitcast.53, f32[2048]{0:T(1024)S(1)} %bitcast.54, f32[2048]{0:T(1024)S(1)} %bitcast.55, f32[2048]{0:T(1024)S(1)} %bitcast.56, ...), kind=kOutput, calls=%fused_computation.130 | convolution fusion | flops 822149120 | bytes 987136 | tf_op jit(solution)/shard_map/while/body/eval_jaxpr/dot_general | solution.py:60
  57.3 3.1 %collective-permute-done.5 = f32[64,2048]{1,0:T(8,128)S(1)} collective-permute-done((f32[64,2048]{1,0:T(8,128)S(1)}, f32[64,2048]{1,0:T(8,128)S(1)}, u32[]{:S(2)}, u32[]{:S(2)}) %collective-permute-start.5) | collective-permute-done | bytes 524320 | tf_op jit(solution)/shard_map/ppermute | solution.py:14
  60.4 5.7 %fusion.134 = f32[512,64]{0,1:T(8,128)S(1)} fusion(f32[512,64]{0,1:T(8,128)S(1)} %fusion.131, f32[64,2048]{1,0:T(8,128)S(1)} %collective-permute-done.5, f32[2048]{0:T(1024)S(1)} %bitcast.60, f32[2048]{0:T(1024)S(1)} %bitcast.61, f32[2048]{0:T(1024)S(1)} %bitcast.62, f32[2048]{0:T(1024)S(1)} %bitcast.63, f32[2048]{0:T(1024)S(1)} %bitcast.64, ...), kind=kOutput, calls=%fused_computation.131 | convolution fusion | flops 822116352 | bytes 856064 | tf_op jit(solution)/shard_map/dot_general | solution.py:60
  66.1 0.3 fusion.151
  66.3 57.7 %psum.7 = f32[64,64]{0,1:T(8,128)S(1)} all-reduce(f32[64,64]{0,1:T(8,128)S(1)} %fusion.151), channel_id=1, replica_groups=mesh['grp'=2,'row'=4,'col'=2,'sub'=2] {'row','col','sub'}, use_global_device_ids=true, to_apply=%region_1.2 | all-reduce | flops 4096 | bytes 32768 | tf_op jit(solution)/shard_map/psum | solution.py:107
  124.0 0.1 copy.10
  124.1 5.8 %cholesky.16 = f32[64,64]{1,0:T(8,128)S(1)} custom-call(f32[64,64]{1,0:T(8,128)S(1)} %fusion.138), custom_call_target="Cholesky" | custom-call | tf_op jit(solution)/shard_map/jit(cholesky)/cholesky | solution.py:108
  129.9 0.6 compare_reduce_fusion
  130.6 0.7 multiply_bitcast_fusion
  131.3 4.9 %custom-call.7 = f32[1,64,64]{1,2,0:T(8,128)S(1)} custom-call(f32[1,64,64]{2,1,0:T(8,128)S(1)} %get-tuple-element.74), custom_call_target="InvertDiagBlocksLowerTriangular" | custom-call | tf_op jit(solution)/shard_map/jit(_solve_triangular)/triangular_solve | solution.py:109
  136.2 1.0 convolution_multiply_fusion
  137.1 0.7 copy.11
  (13 shorter events, 0.3 us)
Async XLA Ops:
  0.6 12.6 %copy-start.1 = (s32[512]{0:T(512)S(1)}, s32[512]{0:T(512)}, u32[]{:S(2)}) copy-start(s32[512]{0:T(512)} %param.4) | copy-start | bytes 6148
  0.6 12.6 %copy-start = (f32[512]{0:T(512)S(1)}, f32[512]{0:T(512)}, u32[]{:S(2)}) copy-start(f32[512]{0:T(512)} %param.5) | copy-start | bytes 6148
  0.7 12.7 %copy-start.2 = (f32[64]{0:T(128)S(1)}, f32[64]{0:T(128)}, u32[]{:S(2)}) copy-start(f32[64]{0:T(128)} %param.6) | copy-start | bytes 772
  9.6 36.8 %collective-permute-start.3 = (f32[64,2048]{1,0:T(8,128)S(1)}, f32[64,2048]{1,0:T(8,128)S(1)}, u32[]{:S(2)}, u32[]{:S(2)}) collective-permute-start(f32[64,2048]{1,0:T(8,128)S(1)} %all_gather.7), channel_id=1, source_target_pairs={{0,12},{4,0},{8,4},{12,8},{1,13},{5,1},{9,5},{13,9},{2,14},{6,2},{... | collective-permute-start | bytes 1572872 | tf_op jit(solution)/shard_map/while/body/eval_jaxpr/ppermute | solution.py:14
  13.2 32.9 %collective-permute-start.1 = (f32[64,2048]{1,0:T(8,128)S(1)}, f32[64,2048]{1,0:T(8,128)S(1)}, u32[]{:S(2)}, u32[]{:S(2)}) collective-permute-start(f32[64,2048]{1,0:T(8,128)S(1)} %all_gather.7), channel_id=1, source_target_pairs={{0,4},{4,8},{8,12},{12,0},{1,5},{5,9},{9,13},{13,1},{2,6},{6,10},{... | collective-permute-start | bytes 1572872 | tf_op jit(solution)/shard_map/while/body/eval_jaxpr/ppermute | solution.py:14
  18.8 22.8 %collective-permute-start.2 = (f32[7,2048]{1,0:T(8,128)S(1)}, f32[7,2048]{1,0:T(8,128)S(1)}, u32[]{:S(2)}, u32[]{:S(2)}) collective-permute-start(f32[7,2048]{1,0:T(8,128)S(1)} %all_gather.6), channel_id=1, source_target_pairs={{0,12},{4,0},{8,4},{12,8},{1,13},{5,1},{9,5},{13,9},{2,14},{6,2},{... | collective-permute-start | bytes 172040 | tf_op jit(solution)/shard_map/while/body/eval_jaxpr/ppermute | solution.py:14
  22.6 17.3 %collective-permute-start = (f32[7,2048]{1,0:T(8,128)S(1)}, f32[7,2048]{1,0:T(8,128)S(1)}, u32[]{:S(2)}, u32[]{:S(2)}) collective-permute-start(f32[7,2048]{1,0:T(8,128)S(1)} %all_gather.6), channel_id=1, source_target_pairs={{0,4},{4,8},{8,12},{12,0},{1,5},{5,9},{9,13},{13,1},{2,6},{6,10},{... | collective-permute-start | bytes 172040 | tf_op jit(solution)/shard_map/while/body/eval_jaxpr/ppermute | solution.py:14
  40.0 6.1 %collective-permute-start.4 = (f32[7,2048]{1,0:T(8,128)S(1)}, f32[7,2048]{1,0:T(8,128)S(1)}, u32[]{:S(2)}, u32[]{:S(2)}) collective-permute-start(f32[7,2048]{1,0:T(8,128)S(1)} %collective-permute-done), channel_id=1, source_target_pairs={{0,4},{4,8},{8,12},{12,0},{1,5},{5,9},{9,13},{13,1},{2,6},{6,10},{... | collective-permute-start | bytes 172040 | tf_op jit(solution)/shard_map/ppermute | solution.py:14
  46.1 14.3 %collective-permute-start.5 = (f32[64,2048]{1,0:T(8,128)S(1)}, f32[64,2048]{1,0:T(8,128)S(1)}, u32[]{:S(2)}, u32[]{:S(2)}) collective-permute-start(f32[64,2048]{1,0:T(8,128)S(1)} %collective-permute-done.1), channel_id=1, source_target_pairs={{0,4},{4,8},{8,12},{12,0},{1,5},{5,9},{9,13},{13,1},{2,6},{6,10},{... | collective-permute-start | bytes 1572872 | tf_op jit(solution)/shard_map/ppermute | solution.py:14
where the time goes:
time: 138 us
  blocking collectives  71.9 us (52%)
  matrix products  23.2 us (17%)
  waiting for transfers between devices  19.4 us (14%)
  other arithmetic  12.3 us (9%)
  starting transfers between devices  9.3 us (7%)
    psum x1, blocking collectives, per_device(): gram_matrix = lax.psum(local_gram, ('row', 'col', 'sub'))  57.7 us
    dot_general x4, matrix products, source_block(): jnp.dot(columns, kernel, precision=lax.Precision.HIGHEST, preferred_eleme...  22 us
    ppermute x6, waiting for transfers between devices, from_behind(): lax.ppermute(shard, axis, [(i, (i + by) % count) for i in range(count)])  19.4 us
    ppermute x6, starting transfers between devices, from_behind(): lax.ppermute(shard, axis, [(i, (i + by) % count) for i in range(count)])  9.3 us
    all_gather x1, blocking collectives, per_device(): lax.all_gather(test_matrix, ('col', 'sub'), axis=1, tiled=True)  8.96 us
    another operation x3, other arithmetic, per_device(): cholesky_low = jnp.linalg.cholesky(gram_matrix)  6.52 us
    all_gather x1, blocking collectives, per_device(): lax.all_gather(targets, ('col', 'sub'), axis=1, tiled=True)  5.25 us
    another operation x1, other arithmetic, per_device(): solved = jax.scipy.linalg.solve_triangular(cholesky_low, sketch, lower=True)  4.9 us
  transfers between devices with their start and end apart: 6, of which 3 were waited for; matrix products, arithmetic and copies ran while one was open for 12% of the time, Pallas kernels for 0%

commit v1 on v0

--- a/solution.py
+++ b/solution.py
@@ -104,7 +104,7 @@
     local_gram = jnp.dot(
         sketch, sketch.T, precision=lax.Precision.HIGHEST, preferred_element_type=jnp.float32
     )
-    gram_matrix = lax.psum(local_gram, ("row", "col", "sub"))
+    gram_matrix = lax.psum(lax.psum(local_gram, ("col", "sub")), "row")
     cholesky_low = jnp.linalg.cholesky(gram_matrix)
     solved = jax.scipy.linalg.solve_triangular(cholesky_low, sketch, lower=True)
     filament_total = (

time: 138 us -> 107 us (0.78)
  blocking collectives: 71.9 us -> 40.9 us
    psum x1 -> x2, blocking collectives: 57.7 us -> 26.7 us  [per_device(): gram_matrix = lax.psum(lax.psum(local_gram, ('col', 'sub')), 'row')]
  transfers between devices with their start and end apart: 6 -> 6, of which waited for: 3 -> 3; matrix products, arithmetic and copies ran while one was open for 12% -> 16% of each run, Pallas kernels for 0% -> 0%
where the time goes in v1:
time: 107 us
  blocking collectives  40.9 us (38%)
  matrix products  23.2 us (22%)
  waiting for transfers between devices  19.4 us (18%)
  other arithmetic  12.3 us (11%)
  starting transfers between devices  9.3 us (9%)
    psum x2, blocking collectives, per_device(): gram_matrix = lax.psum(lax.psum(local_gram, ('col', 'sub')), 'row')  26.7 us
    dot_general x4, matrix products, source_block(): jnp.dot(columns, kernel, precision=lax.Precision.HIGHEST, preferred_eleme...  22 us
    ppermute x6, waiting for transfers between devices, from_behind(): lax.ppermute(shard, axis, [(i, (i + by) % count) for i in range(count)])  19.4 us
    ppermute x6, starting transfers between devices, from_behind(): lax.ppermute(shard, axis, [(i, (i + by) % count) for i in range(count)])  9.3 us
    all_gather x1, blocking collectives, per_device(): lax.all_gather(test_matrix, ('col', 'sub'), axis=1, tiled=True)  8.96 us
    another operation x3, other arithmetic, per_device(): cholesky_low = jnp.linalg.cholesky(gram_matrix)  6.52 us
    all_gather x1, blocking collectives, per_device(): lax.all_gather(targets, ('col', 'sub'), axis=1, tiled=True)  5.25 us
    another operation x1, other arithmetic, per_device(): solved = jax.scipy.linalg.solve_triangular(cholesky_low, sketch, lower=True)  4.9 us
  transfers between devices with their start and end apart: 6, of which 3 were waited for; matrix products, arithmetic and copies ran while one was open for 16% of the time, Pallas kernels for 0%

profile of v1, /device:TPU:0, one launch (start us, length us, event | category | flops | bytes accessed | tf_op | source)
XLA Modules:
  0.0 106.9 jit_solution(14736986049422566341)
XLA Ops:
  0.6 0.0 copy-start.1
  0.7 9.0 %all_gather.7 = f32[64,2048]{1,0:T(8,128)S(1)} all-gather(f32[64,512]{1,0:T(8,128)} %param.7), channel_id=1, replica_groups=mesh['grp'=2,'row'=4,'col'=2,'sub'=2] {'col','sub'}, dimensions={1}, use_global_device_ids=true | all-gather | bytes 655360 | tf_op jit(solution)/shard_map/all_gather | solution.py:86
  9.6 3.6 %collective-permute-start.3 = (f32[64,2048]{1,0:T(8,128)S(1)}, f32[64,2048]{1,0:T(8,128)S(1)}, u32[]{:S(2)}, u32[]{:S(2)}) collective-permute-start(f32[64,2048]{1,0:T(8,128)S(1)} %all_gather.7), channel_id=1, source_target_pairs={{0,12},{4,0},{8,4},{12,8},{1,13},{5,1},{9,5},{13,9},{2,14},{6,2},{... | collective-permute-start | bytes 1572872 | tf_op jit(solution)/shard_map/while/body/eval_jaxpr/ppermute | solution.py:14
  13.2 0.0 collective-permute-start.1
  13.2 0.1 fusion.146
  13.3 0.0 copy-done.2
  13.3 0.1 select_reduce_fusion
  13.5 5.2 %all_gather.6 = f32[7,2048]{1,0:T(8,128)S(1)} all-gather(f32[7,512]{1,0:T(8,128)S(1)} %stack.27), channel_id=1, replica_groups=mesh['grp'=2,'row'=4,'col'=2,'sub'=2] {'col','sub'}, dimensions={1}, use_global_device_ids=true | all-gather | bytes 71680 | tf_op jit(solution)/shard_map/all_gather | solution.py:85
  18.8 3.8 %collective-permute-start.2 = (f32[7,2048]{1,0:T(8,128)S(1)}, f32[7,2048]{1,0:T(8,128)S(1)}, u32[]{:S(2)}, u32[]{:S(2)}) collective-permute-start(f32[7,2048]{1,0:T(8,128)S(1)} %all_gather.6), channel_id=1, source_target_pairs={{0,12},{4,0},{8,4},{12,8},{1,13},{5,1},{9,5},{13,9},{2,14},{6,2},{... | collective-permute-start | bytes 172040 | tf_op jit(solution)/shard_map/while/body/eval_jaxpr/ppermute | solution.py:14
  22.6 0.0 collective-permute-start
  22.6 5.4 %fusion.54 = f32[512,64]{0,1:T(8,128)S(1)} fusion(f32[64,2048]{1,0:T(8,128)S(1)} %all_gather.7, f32[512]{0:T(512)S(1)} %mul.293, f32[2048]{0:T(1024)S(1)} %bitcast.74, f32[512]{0:T(512)S(1)} %get-tuple-element.81, f32[2048]{0:T(1024)S(1)} %bitcast.75, f32[512]{0:T(512)S(1)} %get-tuple-element.79, f32[2048]{0:T(1024)S(1)} %bitcast.76, ...), kind=kOutput, calls=%fused_computation.54 | convolution fusion | flops 822083584 | bytes 724992 | tf_op jit(solution)/shard_map/dot_general | solution.py:60
  28.0 11.9 %collective-permute-done = f32[7,2048]{1,0:T(8,128)S(1)} collective-permute-done((f32[7,2048]{1,0:T(8,128)S(1)}, f32[7,2048]{1,0:T(8,128)S(1)}, u32[]{:S(2)}, u32[]{:S(2)}) %collective-permute-start) | collective-permute-done | bytes 57376 | tf_op jit(solution)/shard_map/while/body/eval_jaxpr/ppermute | solution.py:14
  40.0 1.6 %collective-permute-start.4 = (f32[7,2048]{1,0:T(8,128)S(1)}, f32[7,2048]{1,0:T(8,128)S(1)}, u32[]{:S(2)}, u32[]{:S(2)}) collective-permute-start(f32[7,2048]{1,0:T(8,128)S(1)} %collective-permute-done), channel_id=1, source_target_pairs={{0,4},{4,8},{8,12},{12,0},{1,5},{5,9},{9,13},{13,1},{2,6},{6,10},{... | collective-permute-start | bytes 172040 | tf_op jit(solution)/shard_map/ppermute | solution.py:14
  41.6 0.0 collective-permute-done.2
  41.6 4.4 %collective-permute-done.4 = f32[7,2048]{1,0:T(8,128)S(1)} collective-permute-done((f32[7,2048]{1,0:T(8,128)S(1)}, f32[7,2048]{1,0:T(8,128)S(1)}, u32[]{:S(2)}, u32[]{:S(2)}) %collective-permute-start.4) | collective-permute-done | bytes 57376 | tf_op jit(solution)/shard_map/ppermute | solution.py:14
  46.1 0.0 collective-permute-done.1
  46.1 0.2 collective-permute-start.5
  46.4 0.0 collective-permute-done.3
  46.4 5.5 %fusion.18 = f32[512,64]{0,1:T(8,128)S(1)} fusion(f32[64,2048]{1,0:T(8,128)S(1)} %collective-permute-done.3, f32[2048]{0:T(1024)S(1)} %bitcast.67, f32[2048]{0:T(1024)S(1)} %bitcast.68, f32[2048]{0:T(1024)S(1)} %bitcast.69, f32[2048]{0:T(1024)S(1)} %bitcast.70, f32[2048]{0:T(1024)S(1)} %bitcast.71, f32[2048]{0:T(1024)S(1)} %bitcast.72, ...), kind=kOutput, calls=%fused_computation.18 | convolution fusion | flops 822083584 | bytes 724992 | tf_op jit(solution)/shard_map/while/body/eval_jaxpr/dot_general | solution.py:60
  51.9 5.5 %fusion.131 = f32[512,64]{0,1:T(8,128)S(1)} fusion(f32[512,64]{0,1:T(8,128)S(1)} %fusion.18, f32[512,64]{0,1:T(8,128)S(1)} %fusion.54, f32[64,2048]{1,0:T(8,128)S(1)} %collective-permute-done.1, f32[2048]{0:T(1024)S(1)} %bitcast.53, f32[2048]{0:T(1024)S(1)} %bitcast.54, f32[2048]{0:T(1024)S(1)} %bitcast.55, f32[2048]{0:T(1024)S(1)} %bitcast.56, ...), kind=kOutput, calls=%fused_computation.130 | convolution fusion | flops 822149120 | bytes 987136 | tf_op jit(solution)/shard_map/while/body/eval_jaxpr/dot_general | solution.py:60
  57.3 3.1 %collective-permute-done.5 = f32[64,2048]{1,0:T(8,128)S(1)} collective-permute-done((f32[64,2048]{1,0:T(8,128)S(1)}, f32[64,2048]{1,0:T(8,128)S(1)}, u32[]{:S(2)}, u32[]{:S(2)}) %collective-permute-start.5) | collective-permute-done | bytes 524320 | tf_op jit(solution)/shard_map/ppermute | solution.py:14
  60.4 5.7 %fusion.134 = f32[512,64]{0,1:T(8,128)S(1)} fusion(f32[512,64]{0,1:T(8,128)S(1)} %fusion.131, f32[64,2048]{1,0:T(8,128)S(1)} %collective-permute-done.5, f32[2048]{0:T(1024)S(1)} %bitcast.60, f32[2048]{0:T(1024)S(1)} %bitcast.61, f32[2048]{0:T(1024)S(1)} %bitcast.62, f32[2048]{0:T(1024)S(1)} %bitcast.63, f32[2048]{0:T(1024)S(1)} %bitcast.64, ...), kind=kOutput, calls=%fused_computation.131 | convolution fusion | flops 822116352 | bytes 856064 | tf_op jit(solution)/shard_map/dot_general | solution.py:60
  66.1 0.3 fusion.151
  66.3 10.3 %psum.14 = f32[64,64]{0,1:T(8,128)S(1)} all-reduce(f32[64,64]{0,1:T(8,128)S(1)} %fusion.151), channel_id=1, replica_groups=mesh['grp'=2,'row'=4,'col'=2,'sub'=2] {'col','sub'}, use_global_device_ids=true, to_apply=%region_1.2 | all-reduce | flops 4096 | bytes 32768 | tf_op jit(solution)/shard_map/psum | solution.py:107
  76.6 16.5 %psum.15 = f32[64,64]{0,1:T(8,128)S(1)} all-reduce(f32[64,64]{0,1:T(8,128)S(1)} %psum.14), channel_id=1, replica_groups=mesh['grp'=2,'row'=4,'col'=2,'sub'=2] {'row'}, use_global_device_ids=true, to_apply=%region_2.3 | all-reduce | flops 4096 | bytes 32768 | tf_op jit(solution)/shard_map/psum | solution.py:107
  93.1 0.1 copy.10
  93.2 5.8 %cholesky.16 = f32[64,64]{1,0:T(8,128)S(1)} custom-call(f32[64,64]{1,0:T(8,128)S(1)} %fusion.138), custom_call_target="Cholesky" | custom-call | tf_op jit(solution)/shard_map/jit(cholesky)/cholesky | solution.py:108
  99.1 0.6 compare_reduce_fusion
  99.7 0.7 multiply_bitcast_fusion
  100.4 4.9 %custom-call.7 = f32[1,64,64]{1,2,0:T(8,128)S(1)} custom-call(f32[1,64,64]{2,1,0:T(8,128)S(1)} %get-tuple-element.74), custom_call_target="InvertDiagBlocksLowerTriangular" | custom-call | tf_op jit(solution)/shard_map/jit(_solve_triangular)/triangular_solve | solution.py:109
  105.3 1.0 convolution_multiply_fusion
  106.2 0.7 copy.11
  (14 shorter events, 0.3 us)
Async XLA Ops:
  0.6 12.6 %copy-start.1 = (s32[512]{0:T(512)S(1)}, s32[512]{0:T(512)}, u32[]{:S(2)}) copy-start(s32[512]{0:T(512)} %param.4) | copy-start | bytes 6148
  0.6 12.6 %copy-start = (f32[512]{0:T(512)S(1)}, f32[512]{0:T(512)}, u32[]{:S(2)}) copy-start(f32[512]{0:T(512)} %param.5) | copy-start | bytes 6148
  0.7 12.7 %copy-start.2 = (f32[64]{0:T(128)S(1)}, f32[64]{0:T(128)}, u32[]{:S(2)}) copy-start(f32[64]{0:T(128)} %param.6) | copy-start | bytes 772
  9.6 36.8 %collective-permute-start.3 = (f32[64,2048]{1,0:T(8,128)S(1)}, f32[64,2048]{1,0:T(8,128)S(1)}, u32[]{:S(2)}, u32[]{:S(2)}) collective-permute-start(f32[64,2048]{1,0:T(8,128)S(1)} %all_gather.7), channel_id=1, source_target_pairs={{0,12},{4,0},{8,4},{12,8},{1,13},{5,1},{9,5},{13,9},{2,14},{6,2},{... | collective-permute-start | bytes 1572872 | tf_op jit(solution)/shard_map/while/body/eval_jaxpr/ppermute | solution.py:14
  13.2 32.9 %collective-permute-start.1 = (f32[64,2048]{1,0:T(8,128)S(1)}, f32[64,2048]{1,0:T(8,128)S(1)}, u32[]{:S(2)}, u32[]{:S(2)}) collective-permute-start(f32[64,2048]{1,0:T(8,128)S(1)} %all_gather.7), channel_id=1, source_target_pairs={{0,4},{4,8},{8,12},{12,0},{1,5},{5,9},{9,13},{13,1},{2,6},{6,10},{... | collective-permute-start | bytes 1572872 | tf_op jit(solution)/shard_map/while/body/eval_jaxpr/ppermute | solution.py:14
  18.8 22.8 %collective-permute-start.2 = (f32[7,2048]{1,0:T(8,128)S(1)}, f32[7,2048]{1,0:T(8,128)S(1)}, u32[]{:S(2)}, u32[]{:S(2)}) collective-permute-start(f32[7,2048]{1,0:T(8,128)S(1)} %all_gather.6), channel_id=1, source_target_pairs={{0,12},{4,0},{8,4},{12,8},{1,13},{5,1},{9,5},{13,9},{2,14},{6,2},{... | collective-permute-start | bytes 172040 | tf_op jit(solution)/shard_map/while/body/eval_jaxpr/ppermute | solution.py:14
  22.6 17.3 %collective-permute-start = (f32[7,2048]{1,0:T(8,128)S(1)}, f32[7,2048]{1,0:T(8,128)S(1)}, u32[]{:S(2)}, u32[]{:S(2)}) collective-permute-start(f32[7,2048]{1,0:T(8,128)S(1)} %all_gather.6), channel_id=1, source_target_pairs={{0,4},{4,8},{8,12},{12,0},{1,5},{5,9},{9,13},{13,1},{2,6},{6,10},{... | collective-permute-start | bytes 172040 | tf_op jit(solution)/shard_map/while/body/eval_jaxpr/ppermute | solution.py:14
  40.0 6.1 %collective-permute-start.4 = (f32[7,2048]{1,0:T(8,128)S(1)}, f32[7,2048]{1,0:T(8,128)S(1)}, u32[]{:S(2)}, u32[]{:S(2)}) collective-permute-start(f32[7,2048]{1,0:T(8,128)S(1)} %collective-permute-done), channel_id=1, source_target_pairs={{0,4},{4,8},{8,12},{12,0},{1,5},{5,9},{9,13},{13,1},{2,6},{6,10},{... | collective-permute-start | bytes 172040 | tf_op jit(solution)/shard_map/ppermute | solution.py:14
  46.1 14.3 %collective-permute-start.5 = (f32[64,2048]{1,0:T(8,128)S(1)}, f32[64,2048]{1,0:T(8,128)S(1)}, u32[]{:S(2)}, u32[]{:S(2)}) collective-permute-start(f32[64,2048]{1,0:T(8,128)S(1)} %collective-permute-done.1), channel_id=1, source_target_pairs={{0,4},{4,8},{8,12},{12,0},{1,5},{5,9},{9,13},{13,1},{2,6},{6,10},{... | collective-permute-start | bytes 1572872 | tf_op jit(solution)/shard_map/ppermute | solution.py:14
